TPU v7x, 256 devices: a whole 4x4x8 slice. The times are simulated.
256 devices in a mesh: bin: 8 (over x, y_hi), nuis: 32 (over z, y_lo, core).
Axes of the slice: x: 4, y: 4 (y_hi: 2, y_lo: 2; y = y_hi * 2 + y_lo), z: 8, core: 2. Of those that a mesh axis runs over, the one named last changes fastest.
Arguments:
- derivative: bfloat16 [16, 4, 4, 8, 3072], P('bin', None, None, None, 'nuis'), may hold values from -6 to 6
- group_ids: int32 [3072], P('nuis'), may hold values from 0 to 7
- group_scale: float32 [8], replicated, may hold values from 0.5 to 2
- plane_coupling: float32 [2, 16], P(None, 'bin'), may hold values from 0.1 to 0.9
- band_second: float32 [3, 4], replicated, may hold values from 0.1 to 1
- band_third: float32 [3, 4], replicated, may hold values from 0.1 to 1
- band_offset: int32 [8], replicated, may hold values from -1 to 1, as said below
- band_width: int32 [8], replicated, may hold values from 1 to 3
- expected: float32 [64, 16, 4, 4, 8], P(None, 'bin'), may hold values from 0.5 to 20
Outputs:
- fisher: float32 [64, 3072, 3072], P('bin', 'nuis')
Inputs may be any that keep to these rules, and one draw needn't show every extreme that they name: band_offset + band_width - 1 is at most 1 in every row, so each row reads only its own bin and the two beside it.
All inputs are finite; a program needn't handle non-finite values.
Results may differ from a plain program's by a relative error of at most 0.0026.
Values may be sent and summed in bfloat16 or wider, within the bound.
A program may use at most 64 MiB of HBM per device.

v0:
```python
import jax
import jax.numpy as jnp
from jax import lax
from jax.sharding import PartitionSpec as P

B2 = 4
B3 = 4
B4 = 8


def padded_2(cells, sides, width):
    for axis, dim in sides:
        count = lax.axis_size(axis)
        ends = count - 1
        head = lax.slice_in_dim(cells, 0, width, axis=dim)
        tail = lax.slice_in_dim(cells, cells.shape[dim] - width, cells.shape[dim], axis=dim)
        cells = jnp.concatenate(
            [
                lax.ppermute(tail, axis, [(i, (i + 1) % count) for i in range(ends)]),
                cells,
                lax.ppermute(head, axis, [((i + 1) % count, i) for i in range(ends)]),
            ],
            axis=dim,
        )
    return cells


def banded(band_rows, count):
    row_index = jnp.arange(count)[:, None]
    col_index = jnp.arange(count)[None, :]
    matrix = jnp.where(col_index == row_index - 1, band_rows[0][:, None], jnp.float32(0.0))
    matrix = matrix + jnp.where(col_index == row_index, band_rows[1][:, None], jnp.float32(0.0))
    matrix = matrix + jnp.where(col_index == row_index + 1, band_rows[2][:, None], jnp.float32(0.0))
    return matrix


def local_operator(band_second, band_third, band_offset, band_width):
    second_matrix = banded(band_second, band_second.shape[1])
    third_matrix = banded(band_third, band_third.shape[1])
    count = band_offset.shape[0]
    row_index = jnp.arange(count, dtype=jnp.int32)[:, None]
    col_index = jnp.arange(count, dtype=jnp.int32)[None, :]
    distance = col_index - row_index
    inside = (distance >= band_offset[:, None]) & (
        distance <= band_offset[:, None] + band_width[:, None] - 1
    )
    fourth_matrix = jnp.where(
        inside, 1.0 / band_width[:, None].astype(jnp.float32), jnp.float32(0.0)
    )
    return jnp.kron(second_matrix, jnp.kron(third_matrix, fourth_matrix))


def local(
    derivative,
    group_ids,
    group_scale,
    plane_coupling,
    band_second,
    band_third,
    band_offset,
    band_width,
    expected,
):
    planes = derivative.shape[0]
    own_cols = derivative.shape[4]
    cells = B2 * B3 * B4
    groups = group_scale.shape[0]
    onehot = (group_ids[:, None] == jnp.arange(groups, dtype=jnp.int32)[None, :]).astype(
        jnp.float32
    )
    column_gain = jnp.dot(onehot, group_scale, precision=lax.Precision.HIGHEST)
    padded = padded_2(derivative, (("bin", 0),), 1)
    source = padded.astype(jnp.float32)
    lower_side = plane_coupling[0][:, None, None, None, None]
    upper_side = plane_coupling[1][:, None, None, None, None]
    mixed = source[1:-1] + lower_side * source[:-2] + upper_side * source[2:]
    operator = local_operator(band_second, band_third, band_offset, band_width)
    flattened = mixed.reshape(planes, cells, own_cols)
    smeared = (
        jnp.einsum("ij,ajc->aic", operator, flattened, precision=lax.Precision.HIGHEST)
        * column_gain[None, None, :]
    )
    smeared_panel = smeared.reshape(planes * cells, own_cols).astype(jnp.bfloat16)
    every_point = lax.all_gather(expected, "bin", axis=1, tiled=True)
    share = every_point.shape[0] // lax.axis_size("bin")
    expected_mine = lax.dynamic_slice_in_dim(every_point, lax.axis_index("bin") * share, share, 0)
    point_count = expected_mine.shape[0]
    total_bins = expected_mine.shape[1] * cells
    inverse = 1.0 / expected_mine.reshape(point_count, total_bins) / total_bins
    full_own = lax.all_gather(smeared_panel, "bin", axis=0, tiled=True)
    weighted = (full_own.astype(jnp.float32)[None] * inverse[:, :, None]).astype(jnp.bfloat16)
    return jnp.einsum(
        "krc,rq->kcq",
        weighted,
        lax.all_gather(full_own, "nuis", axis=1, tiled=True),
        preferred_element_type=jnp.float32,
    )


def solution(mesh):
    placed = (
        P("bin", None, None, None, "nuis"),
        P("nuis"),
        P(),
        P(None, "bin"),
        P(),
        P(),
        P(),
        P(),
        P(None, "bin", None, None, None),
    )
    return jax.shard_map(
        local, mesh=mesh, in_specs=placed, out_specs=P("bin", "nuis", None), check_vma=False
    )
```

profile of v0, /device:TPU:1, one launch (start us, length us, event | category | flops | bytes accessed | tf_op | source)
XLA Modules:
  0.0 172.7 jit_solution(4079480639057251630)
XLA Ops:
  6.5 0.8 fusion.14
  7.3 5.6 %collective-permute-start = (bf16[1,4,4,8,96]{4,3,2,1,0:T(8,128)(2,1)S(1)}, bf16[1,4,4,8,96]{4,3,2,1,0:T(8,128)(2,1)S(1)}, u32[]{:S(2)}, u32[]{:S(2)}) collective-permute-start(bf16[1,4,4,8,96]{4,3,2,1,0:T(8,128)(2,1)S(1)} %get-tuple-element.5), channel_id=1, source_target_pairs={{0,32},{32,64},{64,96},{96,128},{128,160},{160,192},{192,224},{1,3... | collective-permute-start | bytes 73736 | tf_op jit(solution)/shard_map/ppermute | solution.py:19
  13.0 1.3 collective-permute-start.1
  14.3 0.7 convert_divide_fusion
  14.9 0.7 add_add_fusion
  15.6 0.8 slice_bitcast_fusion.7
  16.4 0.7 fusion.12
  17.1 0.8 slice_bitcast_fusion.2
  17.9 0.1 select_add_fusion.1
  18.0 0.1 broadcast_multiply_fusion.1
  18.1 0.1 mul.112
  18.2 0.1 broadcast_multiply_fusion
  18.3 0.8 convolution_bitcast_fusion
  19.1 0.2 reshape.325
  19.4 0.9 maximum_convert_fusion
  20.3 0.1 fusion.6
  20.4 0.4 fusion.5
  20.8 32.0 %all_gather.9 = bf16[2048,96]{0,1:T(8,128)(2,1)} all-gather(bf16[256,96]{0,1:T(8,128)(2,1)S(1)} %bitcast.36), channel_id=1, replica_groups=mesh['bin'=8,'nuis'=32] {'bin'}, dimensions={0}, use_global_device_ids=true | all-gather | bytes 442368 | tf_op jit(solution)/shard_map/all_gather | solution.py:90
  52.8 35.0 %all_gather.10 = f32[64,16,4,4,8]{0,4,3,2,1:T(8,128)S(1)} all-gather(f32[64,2,4,4,8]{0,4,3,2,1:T(8,128)} %param.17), channel_id=1, replica_groups=mesh['bin'=8,'nuis'=32] {'bin'}, dimensions={1}, use_global_device_ids=true | all-gather | bytes 589824 | tf_op jit(solution)/shard_map/all_gather | solution.py:84
  87.8 0.3 divide_multiply_fusion
  88.2 0.3 copy.17
  88.4 1.1 convert_element_type.28
  89.5 61.2 %all-gather.2.cloned.1.call-done = bf16[2048,3072]{0,1:T(8,128)(2,1)} async-done(((bf16[2048,96]{0,1:T(8,128)(2,1)}), bf16[2048,3072]{0,1:T(8,128)(2,1)}) %all-gather.2.cloned.1.call-update) | async-done | bytes 12582928 | tf_op jit(solution)/shard_map/all_gather | solution.py:95
  150.7 15.1 %fusion = f32[8,96,3072]{2,1,0:T(8,128)} fusion(bf16[2048,3072]{0,1:T(8,128)(2,1)} %all-gather.2.cloned.1.call-done, f32[8,2048]{1,0:T(8,128)S(1)} %copy.17, f32[2048,96]{0,1:T(8,128)S(1)} %convert_element_type.28), kind=kOutput, calls=%fused_computation | convolution fusion | flops 9666822144 | bytes 22872064 | tf_op jit(solution)/shard_map/krc,rq->kcq/dot_general | solution.py:92
  (8 shorter events, 0.0 us)
Async XLA Ops:
  6.5 11.7 %copy-start = (f32[8]{0:T(128)S(1)}, f32[8]{0:T(128)}, u32[]{:S(2)}) copy-start(f32[8]{0:T(128)} %param.11) | copy-start | bytes 100
  6.5 144.1 %all-gather.2.cloned.1.call-start = ((), (), s32[]{:S(2)}) async-start(), calls=%async_computation | async-start | bytes 12976128 | tf_op jit(solution)/shard_map/all_gather | solution.py:95
  7.3 12.0 %collective-permute-start = (bf16[1,4,4,8,96]{4,3,2,1,0:T(8,128)(2,1)S(1)}, bf16[1,4,4,8,96]{4,3,2,1,0:T(8,128)(2,1)S(1)}, u32[]{:S(2)}, u32[]{:S(2)}) collective-permute-start(bf16[1,4,4,8,96]{4,3,2,1,0:T(8,128)(2,1)S(1)} %get-tuple-element.5), channel_id=1, source_target_pairs={{0,32},{32,64},{64,96},{96,128},{128,160},{160,192},{192,224},{1,3... | collective-permute-start | bytes 73736 | tf_op jit(solution)/shard_map/ppermute | solution.py:19
  13.0 6.4 %collective-permute-start.1 = (bf16[1,4,4,8,96]{4,3,2,1,0:T(8,128)(2,1)S(1)}, bf16[1,4,4,8,96]{4,3,2,1,0:T(8,128)(2,1)S(1)}, u32[]{:S(2)}, u32[]{:S(2)}) collective-permute-start(bf16[1,4,4,8,96]{4,3,2,1,0:T(8,128)(2,1)S(1)} %get-tuple-element.6), channel_id=1, source_target_pairs={{32,0},{64,32},{96,64},{128,96},{160,128},{192,160},{224,192},{33,... | collective-permute-start | bytes 73736 | tf_op jit(solution)/shard_map/ppermute | solution.py:21
Sparse Core Ops, SparseCore 0:
  52.9 97.7 all-gather.1
where the time goes:
time: 173 us
  blocking collectives  67 us (39%)
  waiting for transfers between devices  61.2 us (35%)
  matrix products  16.4 us (9%)
  between operations  13.5 us (8%)
  starting transfers between devices  6.93 us (4%)
  other arithmetic  4.72 us (3%)
  local copies, waits for them, and re-layouts  2.97 us (2%)
    all_gather x1, waiting for transfers between devices, local(): lax.all_gather(full_own, 'nuis', axis=1, tiled=True)  61.2 us
    all_gather x1, blocking collectives, local(): every_point = lax.all_gather(expected, 'bin', axis=1, tiled=True)  35 us
    all_gather x1, blocking collectives, local(): full_own = lax.all_gather(smeared_panel, 'bin', axis=0, tiled=True)  32 us
    dot_general x1, matrix products, local(): jnp.einsum('krc,rq->kcq', weighted, lax.all_gather(full_own, 'nuis', axis...  15.1 us
    ppermute x1, starting transfers between devices, padded_2(): lax.ppermute(tail, axis, [(i, (i + 1) % count) for i in range(ends)])  5.64 us
  transfers between devices with their start and end apart: 3, of which 1 were waited for; matrix products, arithmetic and copies ran while one was open for 4% of the time, Pallas kernels for 0%

commit v1 on v0

v1 whole, which is shorter than its diff:
```python
import functools

import jax
import jax.numpy as jnp
from jax import lax
from jax.experimental import pallas as pl
from jax.experimental.pallas import tpu as pltpu
from jax.sharding import PartitionSpec as P

MESH = pl.DeviceIdType.MESH
NT = (((1,), (1,)), ((), ()))
CELLS = 128
OWN = 96
ROWS = 256
SLOT = {0: 0, 1: 1, -1: 2, 2: 3, -2: 4, 3: 5, -3: 6, 4: 7, -4: 7}
DISTANCE = (0, 1, -1, 2, -2, 3, -3, 4)
GROUPS = ((0, 1), (1, 2), (3, 2), (5, 2), (7, 1))
PART = {"A": (0, 32), "B": (32, 32), "C": (64, 32), "BC": (32, 64)}


def names():
    out = ["halo+", "halo-"]
    out += [f"exp{o}" for o in range(1, 8)]
    out += [f"ap{dx}{dy}" for dx in range(4) for dy in range(4) if dx or dy]
    out += [f"z{s}{w}" for s in range(1, 5) for w in "+-"]
    for s in range(1, 5):
        for w in "+-":
            for h in range(2):
                if s < 4 or h == (0 if w == "+" else 1):
                    out.append(f"az{s}{w}{h}")
    for g in range(5):
        out += [f"by{g}{d}" for d in range(1, 4)] + [f"cx{g}{d}" for d in range(1, 4)]
        out += [f"{n}{g}{w}" for n in ("bx", "bf", "cy", "cf") for w in "+-"]
        out += [f"core{p}{g}" for p in "ABC"]
    return {n: i for i, n in enumerate(out)}


NAMES = names()


def kernel(
    deriv_ref,
    ids_ref,
    scale_ref,
    coupling_ref,
    second_ref,
    third_ref,
    offset_ref,
    width_ref,
    exp_ref,
    out_ref,
    panels,
    weights,
    halo,
    expected,
    send_sem,
    recv_sem,
):
    b = lax.axis_index("bin")
    n = lax.axis_index("nuis")
    x, yh = b // 2, b % 2
    z, yl, c = n // 4, (n // 2) % 2, n % 2
    y = yh * 2 + yl

    def device(dx=0, dy=0, dz=0, dc=0):
        nx, ny, nz = (x + dx + 4) % 4, (y + dy + 4) % 4, (z + dz + 8) % 8
        nc = (c + dc) % 2
        return (nx * 2 + ny // 2, (nz * 2 + ny % 2) * 2 + nc)

    partners = [dict(dx=dx, dy=dy) for dx in range(4) for dy in range(4) if dx or dy]
    partners += [dict(dz=1), dict(dz=-1), dict(dc=1)]
    barrier = pltpu.get_barrier_semaphore()
    for p in partners:
        pl.semaphore_signal(barrier, inc=1, device_id=device(**p), device_id_type=MESH)
    pl.semaphore_wait(barrier, len(partners))

    started = {}
    arrived = set()

    def send(name, src, dst, target):
        i = NAMES[name]
        copy = pltpu.make_async_remote_copy(
            src_ref=src,
            dst_ref=dst,
            send_sem=send_sem.at[i],
            recv_sem=recv_sem.at[i],
            device_id=target,
            device_id_type=MESH,
        )
        copy.start()
        started[name] = copy

    def need(*events):
        for e in events:
            if e not in arrived:
                started[e].wait_recv()
                arrived.add(e)

    nb, pb = (b + 1) % 8, (b + 7) % 8
    send("halo+", deriv_ref.at[pl.ds(CELLS, CELLS)], halo.at[0], (nb, n))
    send("halo-", deriv_ref.at[pl.ds(0, CELLS)], halo.at[1], (pb, n))
    for o in range(1, 8):
        peer = (b + o) % 8
        send(
            f"exp{o}",
            exp_ref.at[pl.ds(pl.multiple_of(peer * 8, 8), 8)],
            expected.at[b],
            (peer, n),
        )
    expected[b] = exp_ref[pl.ds(pl.multiple_of(b * 8, 8), 8), :]

    row = lax.broadcasted_iota(jnp.int32, (CELLS, CELLS), 0)
    col = lax.broadcasted_iota(jnp.int32, (CELLS, CELLS), 1)
    zero = jnp.zeros((CELLS, CELLS), jnp.float32)

    def chain(index, values):
        out = jnp.full((CELLS, CELLS), values[-1])
        for i in range(len(values) - 2, -1, -1):
            out = jnp.where(index == i, values[i], out)
        return out

    def banded(ref, i, j):
        out = zero
        for d in range(3):
            out = jnp.where(j - i == d - 1, chain(i, [ref[d, t] for t in range(4)]), out)
        return out

    r4, c4 = row % 8, col % 8
    offset = chain(r4, [offset_ref[t] for t in range(8)])
    width = chain(r4, [width_ref[t] for t in range(8)])
    inside = (c4 - r4 >= offset) & (c4 - r4 <= offset + width - 1)
    fourth = jnp.where(inside, 1.0 / width.astype(jnp.float32), zero)
    operator = (
        banded(second_ref, row // 32, col // 32)
        * (banded(third_ref, (row // 8) % 4, (col // 8) % 4) * fourth)
    )
    ids = ids_ref[...]
    gain = jnp.zeros((1, OWN), jnp.float32)
    for g in range(8):
        gain = jnp.where(ids == g, scale_ref[g], gain)
    first = deriv_ref[pl.ds(0, CELLS), :].astype(jnp.float32)
    second = deriv_ref[pl.ds(CELLS, CELLS), :].astype(jnp.float32)
    low0 = jnp.where(b == 0, 0.0, coupling_ref[0, 0])
    high1 = jnp.where(b == 7, 0.0, coupling_ref[1, 1])

    need("halo+", "halo-")
    below = halo[0].astype(jnp.float32)
    above = halo[1].astype(jnp.float32)
    mixed = (
        first + low0 * below + coupling_ref[1, 0] * second,
        second + coupling_ref[0, 1] * first + high1 * above,
    )
    for a in range(2):
        panel = lax.dot_general(
            operator,
            mixed[a] * gain,
            (((1,), (0,)), ((), ())),
            precision=lax.Precision.HIGHEST,
            preferred_element_type=jnp.float32,
        )
        panels[0, x, yh, yl, c, :, a * CELLS : (a + 1) * CELLS] = panel.T.astype(jnp.bfloat16)

    def own(slots, part, *place):
        lo, size = PART[part]
        return panels.at[(slots, *place, pl.ds(lo, size))]

    def z_step(s):
        for w, sign in (("+", 1), ("-", -1)):
            if s > 1:
                need(f"z{s - 1}{w}")
            part = "BC" if s < 4 else ("B" if sign == 1 else "C")
            src = SLOT[-sign * (s - 1)]
            dst = SLOT[-sign * s]
            send(
                f"z{s}{w}",
                own(src, part, x, yh, yl, c),
                own(dst, part, x, yh, yl, c),
                device(dz=sign),
            )

    def group(g):
        return pl.ds(*GROUPS[g])

    def group_here(g):
        if 1 <= g:
            need(f"z{g}+", f"z{g}-")

    def first_axis(g):
        group_here(g)
        mine_b = own(group(g), "B", x, yh, yl, c)
        mine_c = own(group(g), "C", x, yh, yl, c)
        for d in (1, 3, 2):
            send(f"by{g}{d}", mine_b, mine_b, device(dy=d))
            send(f"cx{g}{d}", mine_c, mine_c, device(dx=d))

    def second_axis(g):
        need(*[f"by{g}{d}" for d in (1, 3, 2)])
        line = own(group(g), "B", x, slice(None), slice(None), c)
        for w, sign in (("+", 1), ("-", -1)):
            send(f"bx{g}{w}", line, line, device(dx=sign))
        need(*[f"cx{g}{d}" for d in (1, 3, 2)])
        line = own(group(g), "C", slice(None), yh, yl, c)
        for w, sign in (("+", 1), ("-", -1)):
            send(f"cy{g}{w}", line, line, device(dy=sign))

    def far(g):
        for w, sign in (("+", 1), ("-", -1)):
            need(f"bx{g}{w}")
            line = own(group(g), "B", (x - sign + 4) % 4, 0 if sign == 1 else 1, slice(None), c)
            send(f"bf{g}{w}", line, line, device(dx=sign))
        for w, sign in (("+", 1), ("-", -1)):
            need(f"cy{g}{w}")
            oy = (y - sign + 4) % 4
            line = own(group(g), "C", pl.ds(0 if sign == 1 else 2, 2), oy // 2, oy % 2, c)
            send(f"cf{g}{w}", line, line, device(dy=sign))

    def plane_a():
        mine = own(0, "A", x, yh, yl, c)
        for dx in range(4):
            for dy in range(4):
                if dx or dy:
                    send(f"ap{dx}{dy}", mine, mine, device(dx=dx, dy=dy))

    def ring_a(s):
        for h in range(2):
            for w, sign in (("+", 1), ("-", -1)):
                if f"az{s}{w}{h}" not in NAMES:
                    continue
                if s > 1:
                    need(f"az{s - 1}{w}{h}")
                else:
                    need(*[f"ap{dx}{dy}" for dx in range(4) for dy in range(4) if dx or dy])
                place = (pl.ds(2 * h, 2), slice(None), slice(None), c)
                send(
                    f"az{s}{w}{h}",
                    own(SLOT[-sign * (s - 1)], "A", *place),
                    own(SLOT[-sign * s], "A", *place),
                    device(dz=sign),
                )

    def own_a(g):
        if g == 0:
            need(*[f"ap{dx}{dy}" for dx in range(4) for dy in range(4) if dx or dy])
        else:
            need(*[e for e in NAMES if e.startswith(f"az{g}")])

    def share_bc(g):
        need(*[f"bf{g}{w}" for w in "+-"])
        block = own(group(g), "B", slice(None), slice(None), slice(None), c)
        send(f"coreB{g}", block, block, device(dc=1))
        need(*[f"cf{g}{w}" for w in "+-"])
        block = own(group(g), "C", slice(None), slice(None), slice(None), c)
        send(f"coreC{g}", block, block, device(dc=1))

    def share_a(g):
        own_a(g)
        block = own(group(g), "A", slice(None), slice(None), slice(None), c)
        send(f"coreA{g}", block, block, device(dc=1))

    def weigh():
        need(*[f"exp{o}" for o in range(1, 8)])

        def body(t, _):
            inverse = 1.0 / expected[t] / (8.0 * ROWS)
            mine = panels[0, t // 2, t % 2, yl, c].astype(jnp.float32)
            for k in range(8):
                weights[t, pl.ds(k * OWN, OWN), :] = (mine * inverse[k : k + 1, :]).astype(
                    jnp.bfloat16
                )
            return 0

        lax.fori_loop(0, 8, body, 0)

    def multiply(g):
        need(f"coreA{g}", f"coreB{g}", f"coreC{g}")
        start, count = GROUPS[g]
        lhs = jnp.concatenate([weights[t] for t in range(8)], axis=1)
        blocks = []
        for i in range(count):
            blocks.append(
                jnp.concatenate(
                    [panels[start + i, t // 2, t % 2].reshape(4 * OWN, ROWS) for t in range(8)], axis=1
                )
            )
        rhs = blocks[0] if count == 1 else jnp.concatenate(blocks, axis=0)
        step = 384 if count == 1 else 256
        for i in range(count * 384 // step):
            product = lax.dot_general(
                lhs, rhs[i * step : (i + 1) * step], NT, preferred_element_type=jnp.float32
            )
            at = i * step
            while at < (i + 1) * step:
                which, inner = at // 384, at % 384
                size = min(384 - inner, (i + 1) * step - at)
                zz = (z + DISTANCE[start + which] + 8) % 8
                column = pl.multiple_of(zz * 384 + inner, 128)
                out_ref[:, pl.ds(column, size)] = product[:, at - i * step : at - i * step + size]
                at += size

    z_step(1)
    first_axis(0)
    plane_a()
    z_step(2)
    first_axis(1)
    second_axis(0)
    z_step(3)
    first_axis(2)
    ring_a(1)
    far(0)
    second_axis(1)
    share_a(0)
    z_step(4)
    first_axis(3)
    share_bc(0)
    far(1)
    first_axis(4)
    second_axis(2)
    weigh()
    multiply(0)
    ring_a(2)
    share_a(1)
    second_axis(3)
    share_bc(1)
    far(2)
    multiply(1)
    ring_a(3)
    share_a(2)
    second_axis(4)
    share_bc(2)
    far(3)
    multiply(2)
    ring_a(4)
    share_a(3)
    far(4)
    share_bc(3)
    multiply(3)
    share_bc(4)
    share_a(4)
    multiply(4)
    for copy in started.values():
        copy.wait_send()


def local(
    derivative,
    group_ids,
    group_scale,
    plane_coupling,
    band_second,
    band_third,
    band_offset,
    band_width,
    expected,
):
    flat = derivative.reshape(2 * CELLS, OWN)
    every = expected.reshape(64, ROWS)
    smem = pl.BlockSpec(memory_space=pltpu.SMEM)
    vmem = pl.BlockSpec(memory_space=pltpu.VMEM)
    count = len(NAMES)
    out = pl.pallas_call(
        kernel,
        out_shape=jax.ShapeDtypeStruct((8 * OWN, 3072), jnp.float32),
        in_specs=[vmem, vmem, smem, smem, smem, smem, smem, smem, vmem],
        out_specs=vmem,
        scratch_shapes=[
            pltpu.VMEM((8, 4, 2, 2, 2, OWN, ROWS), jnp.bfloat16),
            pltpu.VMEM((8, 8 * OWN, ROWS), jnp.bfloat16),
            pltpu.VMEM((2, CELLS, OWN), jnp.bfloat16),
            pltpu.VMEM((8, 8, ROWS), jnp.float32),
            pltpu.SemaphoreType.DMA((count,)),
            pltpu.SemaphoreType.DMA((count,)),
        ],
        compiler_params=pltpu.CompilerParams(
            collective_id=0, has_side_effects=True, vmem_limit_bytes=40 * 1024 * 1024
        ),
        cost_estimate=pl.CostEstimate(
            flops=2 * 768 * 2048 * 3072, bytes_accessed=10_000_000, transcendentals=0
        ),
        name="fisher",
    )(
        flat,
        group_ids.reshape(1, OWN),
        group_scale,
        plane_coupling,
        band_second,
        band_third,
        band_offset,
        band_width,
        every,
    )
    return out.reshape(8, OWN, 3072)


def solution(mesh):
    placed = (
        P("bin", None, None, None, "nuis"),
        P("nuis"),
        P(),
        P(None, "bin"),
        P(),
        P(),
        P(),
        P(),
        P(None, "bin", None, None, None),
    )
    return jax.shard_map(
        local, mesh=mesh, in_specs=placed, out_specs=P("bin", "nuis", None), check_vma=False
    )
```

time: 173 us -> 72.9 us (0.42)
  blocking collectives: 67 us -> 0 us
  Pallas kernels: 0 us -> 62.5 us
  waiting for transfers between devices: 61.2 us -> 0 us
  matrix products: 16.4 us -> 0 us
  between operations: 13.5 us -> 0.03 us
  local copies, waits for them, and re-layouts: 2.97 us -> 10.2 us
  starting transfers between devices: 6.93 us -> 0 us
  other arithmetic: 4.72 us -> 0 us
    all_gather x2 -> x0, blocking collectives: 67 us -> none  [the longest x1 35 us: local(): every_point = lax.all_gather(expected, 'bin', axis=1, tiled=True)]
    pallas_call x0 -> x1, Pallas kernels: none -> 62.5 us  [local(): pl.pallas_call(kernel, out_shape=jax.ShapeDtypeStruct((8 * OWN, 3072), jn...]
    all_gather x1 -> x0, waiting for transfers between devices: 61.2 us -> none  [local(): lax.all_gather(full_own, 'nuis', axis=1, tiled=True)]
    dot_general x3 -> x0, matrix products: 16.4 us -> none  [the longest x1 15.1 us: local(): jnp.einsum('krc,rq->kcq', weighted, lax.all_gather(full_own, 'nuis', axis...]
    unnamed x2 -> x17, local copies, waits for them, and re-layouts: 0.01 us -> 9.24 us
    ppermute x2 -> x0, starting transfers between devices: 6.93 us -> none  [the longest x1 5.64 us: padded_2(): lax.ppermute(tail, axis, [(i, (i + 1) % count) for i in range(ends)])]
    convert_element_type x2 -> x0, other arithmetic: 1.95 us -> none  [the longest x1 1.07 us: local(): full_own.astype(jnp.float32)[None] * inverse[:, :, None]]
  transfers between devices with their start and end apart: 3 -> 0, of which waited for: 1 -> 0; matrix products, arithmetic and copies ran while one was open for 4% -> 0% of each run, Pallas kernels for 0% -> 0%
where the time goes in v1:
time: 72.9 us; the launch traced here: 72.7 us
  Pallas kernels  62.5 us (86%)
  local copies, waits for them, and re-layouts  10.2 us (14%)
    pallas_call x1, Pallas kernels, local(): pl.pallas_call(kernel, out_shape=jax.ShapeDtypeStruct((8 * OWN, 3072), jn...  62.5 us
    unnamed x17, local copies, waits for them, and re-layouts  9.24 us

profile of v1, /device:TPU:1, one launch (start us, length us, event | category | flops | bytes accessed | tf_op | source)
XLA Modules:
  0.0 72.7 jit_solution(14644039904405174737)
XLA Ops:
  0.0 1.0 %copy.11.exp_ref = f32[64,256]{1,0:T(8,128)S(1)} copy(f32[64,256]{0,1:T(8,128)} %bitcast.7) | data formatting | bytes 131072 | tf_op jit(solution)/shard_map/reshape | solution.py:356
  1.0 0.0 copy-start
  1.0 0.8 %copy-done = bf16[2,4,4,8,96]{4,3,2,1,0:T(8,128)(2,1)S(1)} copy-done((bf16[2,4,4,8,96]{4,3,2,1,0:T(8,128)(2,1)S(1)}, bf16[2,4,4,8,96]{4,3,2,1,0:T(8,128)(2,1)}, u32[]{:S(2)}) %copy-start) | copy-done | bytes 49176
  1.8 0.0 copy-start.1
  1.8 0.7 copy-done.1
  2.5 0.0 copy-start.2
  2.5 0.7 copy-done.2
  3.2 0.0 copy-start.3
  3.2 0.7 copy-done.3
  3.9 0.0 copy-start.4
  3.9 0.7 copy-done.4
  4.5 0.0 copy-start.5
  4.5 0.7 copy-done.5
  5.2 0.0 copy-start.6
  5.2 0.7 copy-done.6
  5.8 0.0 copy-start.7
  5.8 0.7 copy-done.7
  6.5 62.5 %fisher.1 = f32[768,3072]{1,0:T(8,128)S(1)} custom-call(bf16[256,96]{1,0:T(8,128)(2,1)S(1)} %bitcast.5, s32[1,96]{1,0:T(1,128)S(1)} %bitcast.6, f32[8]{0:T(128)S(1)} %copy-done.5, f32[2,2]{1,0:T(2,128)S(1)} %copy-done.3, f32[3,4]{1,0:T(4,128)S(1)} %copy-done.1, f32[3,4]{1,0:T(4,128)S(1)} %copy-done.2, s32[8]{0:T(128)S(1)} %copy-done.6, s32[8]{0:T(128)S(1)} %copy-done.7, ...), custom_call_target="tpu_custom_call" | custom-call | flops 9663676416 | bytes 10000000 | tf_op jit(solution)/shard_map/fisher/pallas_call | solution.py:360
  69.0 3.7 %copy.13 = f32[8,96,3072]{2,1,0:T(8,128)} copy(f32[8,96,3072]{2,1,0:T(8,128)S(1)} %bitcast.4) | data formatting | bytes 18874368
Async XLA Ops:
  1.0 0.8 %copy-start = (bf16[2,4,4,8,96]{4,3,2,1,0:T(8,128)(2,1)S(1)}, bf16[2,4,4,8,96]{4,3,2,1,0:T(8,128)(2,1)}, u32[]{:S(2)}) copy-start(bf16[2,4,4,8,96]{4,3,2,1,0:T(8,128)(2,1)} %param.9) | copy-start | bytes 147460
  1.8 0.7 copy-start.1
  2.5 0.7 copy-start.2
  3.2 0.7 copy-start.3
  3.9 0.7 copy-start.4
  4.5 0.7 copy-start.5
  5.2 0.7 copy-start.6
  5.8 0.7 copy-start.7

commit v2 on v1

v2 whole, which is shorter than its diff:
```python
import functools

import jax
import jax.numpy as jnp
from jax import lax
from jax.experimental import pallas as pl
from jax.experimental.pallas import tpu as pltpu
from jax.sharding import PartitionSpec as P

MESH = pl.DeviceIdType.MESH
NT = (((1,), (1,)), ((), ()))
CELLS = 128
OWN = 96
ROWS = 256
SLOT = {0: 0, 1: 1, -1: 2, 2: 3, -2: 4, 3: 5, -3: 6, 4: 7, -4: 7}
DISTANCE = (0, 1, -1, 2, -2, 3, -3, 4)
GROUPS = ((0, 1), (1, 2), (3, 2), (5, 2), (7, 1))
GROUP_OF = (0, 1, 1, 2, 2, 3, 3, 4)
WIDE = 512
PART = {"A": (0, 32), "B": (32, 32), "C": (64, 32), "BC": (32, 64)}


HEAD = 1536


def events():
    out = ["halo+", "halo-", "exp", "ap"]
    out += [f"z{s}{w}" for s in range(1, 5) for w in "+-"]
    for s in range(1, 5):
        for w in "+-":
            for h in range(2):
                if s < 4 or h == (0 if w == "+" else 1):
                    out.append(f"az{s}{w}{h}")
    for g in range(5):
        out += [f"by{g}", f"cx{g}", f"bf{g}", f"cf{g}"]
        out += [f"{n}{g}{w}" for n in ("bx", "cy") for w in "+-"]
        out += [f"core{p}{g}" for p in "ABC"]
    return {n: i for i, n in enumerate(out)}


EVENTS = events()
DEPARTURES = ["halo+", "halo-", "exp", "ap", "z", "az"]
DEPARTURES += [f"{n}{g}" for n in ("link", "core") for g in range(5)]
DEPARTURES = {n: i for i, n in enumerate(DEPARTURES)}


def slots(i):
    out, at, end = {}, i * WIDE, (i + 1) * WIDE
    while at < end:
        slot, inner = at // 384, at % 384
        out[slot] = (inner, min(384 - inner, end - at))
        at += out[slot][1]
    return out


def product(weights, panels, i):
    lhs = jnp.concatenate([weights[t] for t in range(8)], axis=1)
    blocks = []
    for slot, (inner, size) in slots(i).items():
        block = [panels[slot, t // 2, t % 2].reshape(4 * OWN, ROWS) for t in range(8)]
        blocks.append(jnp.concatenate(block, axis=1)[inner : inner + size])
    return lax.dot_general(
        lhs, jnp.concatenate(blocks, axis=0), NT, preferred_element_type=jnp.float32
    )


def finish(panels, weights, head, out_ref, tail, sems):
    z = lax.div(lax.axis_index("nuis"), 4)
    copies = []

    def write(i, source, first):
        at = first
        for slot, (inner, size) in slots(i).items():
            column = lax.rem(z + (DISTANCE[slot] + 8), 8) * 384 + inner
            copy = pltpu.make_async_copy(
                source.at[:, pl.ds(at, size)],
                out_ref.at[:, pl.ds(pl.multiple_of(column, 128), size)],
                sems.at[len(copies)],
            )
            copy.start()
            copies.append(copy)
            at += size

    for i in range(6):
        if i < HEAD // WIDE:
            write(i, head, i * WIDE)
        else:
            tail[:, i * WIDE - HEAD : (i + 1) * WIDE - HEAD] = product(weights, panels, i)
            write(i, tail, i * WIDE - HEAD)
    for copy in copies:
        copy.wait()


def kernel(
    deriv_in,
    ids_in,
    scale_in,
    coupling_in,
    second_in,
    third_in,
    offset_in,
    width_in,
    exp_in,
    panels,
    weights,
    out_ref,
    halo,
    expected,
    deriv_ref,
    ids_ref,
    scale_ref,
    coupling_ref,
    second_ref,
    third_ref,
    offset_ref,
    width_ref,
    exp_cols,
    exp_ref,
    operator_ref,
    gain_ref,
    in_sem,
    send_sem,
    recv_sem,
):
    b = lax.axis_index("bin")
    n = lax.axis_index("nuis")
    x, yh = lax.div(b, 2), lax.rem(b, 2)
    z, yl, c = lax.div(n, 4), lax.rem(lax.div(n, 2), 2), lax.rem(n, 2)
    y = yh * 2 + yl

    def device(dx=0, dy=0, dz=0, dc=0):
        nx = lax.rem(x + (dx + 4), 4) if dx else x
        ny = lax.rem(y + (dy + 4), 4) if dy else y
        nz = lax.rem(z + (dz + 8), 8) if dz else z
        nc = 1 - c if dc else c
        nyh, nyl = (lax.div(ny, 2), lax.rem(ny, 2)) if dy else (yh, yl)
        return (nx * 2 + nyh, nz * 4 + nyl * 2 + nc)

    inputs = [
        pltpu.make_async_copy(src, dst, in_sem.at[i])
        for i, (src, dst) in enumerate(
            (
                (second_in, second_ref),
                (third_in, third_ref),
                (offset_in, offset_ref),
                (width_in, width_ref),
                (scale_in, scale_ref),
                (ids_in, ids_ref),
                (coupling_in, coupling_ref),
                (exp_in, exp_cols),
                (deriv_in, deriv_ref),
            )
        )
    ]
    for copy in inputs:
        copy.start()

    partners = [dict(dx=dx, dy=dy) for dx in range(4) for dy in range(4) if dx or dy]
    partners += [dict(dz=1), dict(dz=-1), dict(dc=1)]
    barrier = pltpu.get_barrier_semaphore()
    for p in partners:
        pl.semaphore_signal(barrier, inc=1, device_id=device(**p), device_id_type=MESH)

    for copy in inputs[:6]:
        copy.wait()
    row = lax.broadcasted_iota(jnp.int32, (CELLS, CELLS), 0)
    col = lax.broadcasted_iota(jnp.int32, (CELLS, CELLS), 1)
    zero = jnp.zeros((CELLS, CELLS), jnp.float32)

    def chain(index, values):
        out = jnp.full((CELLS, CELLS), values[-1])
        for i in range(len(values) - 2, -1, -1):
            out = jnp.where(index == i, values[i], out)
        return out

    def banded(ref, i, j):
        out = zero
        for d in range(3):
            out = jnp.where(j - i == d - 1, chain(i, [ref[d, t] for t in range(4)]), out)
        return out

    r4, c4 = row & 7, col & 7
    offset = chain(r4, [offset_ref[t] for t in range(8)])
    width = chain(r4, [width_ref[t] for t in range(8)])
    inside = (c4 - r4 >= offset) & (c4 - r4 <= offset + width - 1)
    fourth = jnp.where(inside, 1.0 / width.astype(jnp.float32), zero)
    operator_ref[...] = (
        banded(second_ref, row >> 5, col >> 5)
        * (banded(third_ref, (row >> 3) & 3, (col >> 3) & 3) * fourth)
    )
    ids = ids_ref[...]
    gain = jnp.zeros((1, OWN), jnp.float32)
    for g in range(8):
        gain = jnp.where(ids == g, scale_ref[g], gain)
    gain_ref[...] = gain
    for copy in inputs[6:]:
        copy.wait()
    exp_ref[...] = exp_cols[...].T
    pl.semaphore_wait(barrier, len(partners))

    started = {}
    departed = {}
    arrived = set()

    def rows(count, wide=1):
        return weights.at[pl.ds(0, wide), pl.ds(0, count)]

    def send(event, departure, src, dst, target):
        copy = pltpu.make_async_remote_copy(
            src_ref=src,
            dst_ref=dst,
            send_sem=send_sem.at[DEPARTURES[departure]],
            recv_sem=recv_sem.at[EVENTS[event]],
            device_id=target,
            device_id_type=MESH,
        )
        copy.start()
        started[event] = copy
        departed[departure] = copy

    def empty(semaphore, like):
        pltpu.make_async_copy(like, like, semaphore).wait()

    def need(*events):
        for e in events:
            if e in arrived:
                continue
            arrived.add(e)
            semaphore = recv_sem.at[EVENTS[e]]
            if e == "exp":
                empty(semaphore, expected.at[pl.ds(0, 7)])
            elif e == "ap":
                empty(semaphore, rows(480))
            elif e[:2] in ("by", "cx"):
                empty(semaphore, rows(96 * GROUPS[int(e[2])][1]))
            elif e[:2] in ("bf", "cf"):
                empty(semaphore, rows(128 * GROUPS[int(e[2])][1]))
            else:
                started[e].wait_recv()

    nb, pb = lax.rem(b + 1, 8), lax.rem(b + 7, 8)
    send("halo+", "halo+", deriv_ref.at[pl.ds(CELLS, CELLS)], halo.at[0], (nb, n))
    send("halo-", "halo-", deriv_ref.at[pl.ds(0, CELLS)], halo.at[1], (pb, n))
    first = deriv_ref[pl.ds(0, CELLS), :].astype(jnp.float32)
    second = deriv_ref[pl.ds(CELLS, CELLS), :].astype(jnp.float32)
    low0 = jnp.where(b == 0, 0.0, coupling_ref[0, 0])
    high1 = jnp.where(b == 7, 0.0, coupling_ref[1, 1])

    need("halo+", "halo-")
    below = halo[0].astype(jnp.float32)
    above = halo[1].astype(jnp.float32)
    mixed = (
        first + low0 * below + coupling_ref[1, 0] * second,
        second + coupling_ref[0, 1] * first + high1 * above,
    )
    for a in range(2):
        panel = lax.dot_general(
            operator_ref[...],
            mixed[a] * gain_ref[...],
            (((1,), (0,)), ((), ())),
            precision=lax.Precision.HIGHEST,
            preferred_element_type=jnp.float32,
        )
        panels[0, x, yh, yl, c, :, a * CELLS : (a + 1) * CELLS] = panel.T.astype(jnp.bfloat16)

    def send_expected():
        for o in range(1, 8):
            peer = lax.rem(b + o, 8)
            send(
                "exp",
                "exp",
                exp_ref.at[pl.ds(pl.multiple_of(peer * 8, 8), 8)],
                expected.at[b],
                (peer, n),
            )
        expected[b] = exp_ref[pl.ds(pl.multiple_of(b * 8, 8), 8), :]

    def own(slots, part, *place):
        lo, size = PART[part]
        return panels.at[(slots, *place, pl.ds(lo, size))]

    def z_step(s):
        for w, sign in (("+", 1), ("-", -1)):
            if s > 1:
                need(f"z{s - 1}{w}")
            part = "BC" if s < 4 else ("B" if sign == 1 else "C")
            src = SLOT[-sign * (s - 1)]
            dst = SLOT[-sign * s]
            send(
                f"z{s}{w}",
                "z",
                own(src, part, x, yh, yl, c),
                own(dst, part, x, yh, yl, c),
                device(dz=sign),
            )

    def group(g):
        return pl.ds(*GROUPS[g])

    def group_here(g):
        if 1 <= g:
            need(f"z{g}+", f"z{g}-")

    def first_axis(g):
        group_here(g)
        mine_b = own(group(g), "B", x, yh, yl, c)
        mine_c = own(group(g), "C", x, yh, yl, c)
        for d in (1, 3, 2):
            send(f"by{g}", f"link{g}", mine_b, mine_b, device(dy=d))
            send(f"cx{g}", f"link{g}", mine_c, mine_c, device(dx=d))

    def second_axis(g):
        need(f"by{g}")
        line = own(group(g), "B", x, slice(None), slice(None), c)
        for w, sign in (("+", 1), ("-", -1)):
            send(f"bx{g}{w}", f"link{g}", line, line, device(dx=sign))
        need(f"cx{g}")
        line = own(group(g), "C", slice(None), yh, yl, c)
        for w, sign in (("+", 1), ("-", -1)):
            send(f"cy{g}{w}", f"link{g}", line, line, device(dy=sign))

    def far(g):
        for w, sign in (("+", 1), ("-", -1)):
            need(f"bx{g}{w}")
            line = own(group(g), "B", lax.rem(x + (4 - sign), 4), 0 if sign == 1 else 1, slice(None), c)
            send(f"bf{g}", f"link{g}", line, line, device(dx=sign))
        for w, sign in (("+", 1), ("-", -1)):
            need(f"cy{g}{w}")
            oy = lax.rem(y + (4 - sign), 4)
            line = own(group(g), "C", pl.ds(0 if sign == 1 else 2, 2), lax.div(oy, 2), lax.rem(oy, 2), c)
            send(f"cf{g}", f"link{g}", line, line, device(dy=sign))

    def plane_a():
        mine = own(0, "A", x, yh, yl, c)
        for dx in range(4):
            for dy in range(4):
                if dx or dy:
                    send("ap", "ap", mine, mine, device(dx=dx, dy=dy))

    def ring_a(s, h):
        for w, sign in (("+", 1), ("-", -1)):
            if f"az{s}{w}{h}" not in EVENTS:
                continue
            if s > 1:
                need(f"az{s - 1}{w}{h}")
            else:
                need("ap")
            place = (pl.ds(2 * h, 2), slice(None), slice(None), c)
            send(
                f"az{s}{w}{h}",
                "az",
                own(SLOT[-sign * (s - 1)], "A", *place),
                own(SLOT[-sign * s], "A", *place),
                device(dz=sign),
            )

    def own_a(g):
        if g == 0:
            need("ap")
        else:
            need(*[e for e in EVENTS if e.startswith(f"az{g}")])

    def share_bc(g):
        need(f"bf{g}")
        block = own(group(g), "B", slice(None), slice(None), slice(None), c)
        send(f"coreB{g}", f"core{g}", block, block, device(dc=1))
        need(f"cf{g}")
        block = own(group(g), "C", slice(None), slice(None), slice(None), c)
        send(f"coreC{g}", f"core{g}", block, block, device(dc=1))

    def share_a(g):
        own_a(g)
        block = own(group(g), "A", slice(None), slice(None), slice(None), c)
        send(f"coreA{g}", f"core{g}", block, block, device(dc=1))

    def weigh():
        need("exp")

        def body(t, _):
            inverse = 1.0 / expected[t] / (8.0 * ROWS)
            mine = panels[0, lax.div(t, 2), lax.rem(t, 2), yl, c].astype(jnp.float32)
            for k in range(8):
                weights[t, pl.ds(k * OWN, OWN), :] = (mine * inverse[k : k + 1, :]).astype(
                    jnp.bfloat16
                )
            return 0

        lax.fori_loop(0, 8, body, 0)

    def multiply(i):
        for slot in slots(i):
            need(*[f"core{p}{GROUP_OF[slot]}" for p in "ABC"])
        out_ref[:, i * WIDE : (i + 1) * WIDE] = product(weights, panels, i)

    z_step(1)
    first_axis(0)
    plane_a()
    z_step(2)
    first_axis(1)
    second_axis(0)
    z_step(3)
    ring_a(1, 0)
    first_axis(2)
    ring_a(1, 1)
    second_axis(1)
    far(0)
    send_expected()
    z_step(4)
    first_axis(3)
    share_a(0)
    second_axis(2)
    far(1)
    ring_a(2, 0)
    first_axis(4)
    second_axis(3)
    share_bc(0)
    ring_a(2, 1)
    weigh()
    share_a(1)
    far(2)
    second_axis(4)
    ring_a(3, 0)
    share_bc(1)
    ring_a(3, 1)
    far(3)
    multiply(0)
    share_a(2)
    ring_a(4, 0)
    share_bc(2)
    far(4)
    multiply(1)
    ring_a(4, 1)
    share_a(3)
    share_bc(3)
    multiply(2)
    share_bc(4)
    share_a(4)
    for g in range(5):
        need(*[f"core{p}{g}" for p in "ABC"])
    for d in DEPARTURES:
        semaphore = send_sem.at[DEPARTURES[d]]
        if d == "exp":
            empty(semaphore, expected.at[pl.ds(0, 7)])
        elif d == "ap":
            empty(semaphore, rows(480))
        elif d == "z":
            empty(semaphore, rows(448))
        elif d == "az":
            empty(semaphore, rows(512, 7))
        elif d.startswith("link"):
            empty(semaphore, rows(480, 2 * GROUPS[int(d[4])][1]))
        elif d.startswith("core"):
            empty(semaphore, panels.at[group(int(d[4])), :, :, :, 0])
        else:
            departed[d].wait_send()


def local(
    derivative,
    group_ids,
    group_scale,
    plane_coupling,
    band_second,
    band_third,
    band_offset,
    band_width,
    expected,
):
    flat = derivative.reshape(2 * CELLS, OWN)
    every = expected.transpose(1, 2, 3, 4, 0).reshape(ROWS, 64)
    hbm = pl.BlockSpec(memory_space=pltpu.HBM)
    vmem = pl.BlockSpec(memory_space=pltpu.VMEM)
    made = pl.pallas_call(
        kernel,
        out_shape=[
            pltpu.VMEM((8, 4, 2, 2, 2, OWN, ROWS), jnp.bfloat16),
            pltpu.VMEM((8, 8 * OWN, ROWS), jnp.bfloat16),
            pltpu.VMEM((8 * OWN, HEAD), jnp.float32),
        ],
        in_specs=[hbm] * 9,
        out_specs=[vmem] * 3,
        scratch_shapes=[
            pltpu.VMEM((2, CELLS, OWN), jnp.bfloat16),
            pltpu.VMEM((8, 8, ROWS), jnp.float32),
            pltpu.VMEM((2 * CELLS, OWN), jnp.bfloat16),
            pltpu.VMEM((1, OWN), jnp.int32),
            pltpu.SMEM((8,), jnp.float32),
            pltpu.SMEM((2, 2), jnp.float32),
            pltpu.SMEM((3, 4), jnp.float32),
            pltpu.SMEM((3, 4), jnp.float32),
            pltpu.SMEM((8,), jnp.int32),
            pltpu.SMEM((8,), jnp.int32),
            pltpu.VMEM((ROWS, 64), jnp.float32),
            pltpu.VMEM((64, ROWS), jnp.float32),
            pltpu.VMEM((CELLS, CELLS), jnp.float32),
            pltpu.VMEM((1, OWN), jnp.float32),
            pltpu.SemaphoreType.DMA((9,)),
            pltpu.SemaphoreType.DMA((len(DEPARTURES),)),
            pltpu.SemaphoreType.DMA((len(EVENTS),)),
        ],
        compiler_params=pltpu.CompilerParams(
            collective_id=0, has_side_effects=True, vmem_limit_bytes=16 * 1024 * 1024
        ),
        cost_estimate=pl.CostEstimate(
            flops=2 * 768 * 2048 * HEAD, bytes_accessed=10_000_000, transcendentals=0
        ),
        name="fisher",
    )(
        *[
            pltpu.with_memory_space_constraint(a, pltpu.HBM)
            for a in (
                flat,
                group_ids.reshape(1, OWN),
                group_scale,
                plane_coupling,
                band_second,
                band_third,
                band_offset,
                band_width,
                every,
            )
        ]
    )
    out = pl.pallas_call(
        finish,
        out_shape=jax.ShapeDtypeStruct((8 * OWN, 3072), jnp.float32),
        in_specs=[vmem] * 3,
        out_specs=hbm,
        scratch_shapes=[
            pltpu.VMEM((8 * OWN, 3072 - HEAD), jnp.float32),
            pltpu.SemaphoreType.DMA((16,)),
        ],
        compiler_params=pltpu.CompilerParams(vmem_limit_bytes=16 * 1024 * 1024),
        cost_estimate=pl.CostEstimate(
            flops=2 * 768 * 2048 * (3072 - HEAD), bytes_accessed=10_000_000, transcendentals=0
        ),
        name="finish",
    )(*[pltpu.with_memory_space_constraint(a, pltpu.VMEM) for a in made])
    return out.reshape(8, OWN, 3072)


def solution(mesh):
    placed = (
        P("bin", None, None, None, "nuis"),
        P("nuis"),
        P(),
        P(None, "bin"),
        P(),
        P(),
        P(),
        P(),
        P(None, "bin", None, None, None),
    )
    return jax.shard_map(
        local, mesh=mesh, in_specs=placed, out_specs=P("bin", "nuis", None), check_vma=False
    )
```

time: 72.9 us -> 57.3 us (0.79)
  local copies, waits for them, and re-layouts: 10.2 us -> 0 us
  Pallas kernels: 62.5 us -> 57.2 us
    unnamed x17 -> x0, local copies, waits for them, and re-layouts: 9.24 us -> none
    pallas_call x1 -> x2, Pallas kernels: 62.5 us -> 57.2 us  [the longest x1 50.8 us: local(): pl.pallas_call(kernel, out_shape=[pltpu.VMEM((8, 4, 2, 2, 2, OWN, ROWS),...]
    reshape x1 -> x0, local copies, waits for them, and re-layouts: 0.98 us -> none  [local(): every = expected.reshape(64, ROWS)]
where the time goes in v2:
time: 57.3 us; the launch traced here: 57.2 us
  Pallas kernels  57.2 us (100%)
    pallas_call x1, Pallas kernels, local(): pl.pallas_call(kernel, out_shape=[pltpu.VMEM((8, 4, 2, 2, 2, OWN, ROWS),...  50.8 us
    pallas_call x1, Pallas kernels, local(): pl.pallas_call(finish, out_shape=jax.ShapeDtypeStruct((8 * OWN, 3072), jn...  6.34 us

profile of v2, /device:TPU:1, one launch (start us, length us, event | category | flops | bytes accessed | tf_op | source)
XLA Modules:
  0.0 57.2 jit_solution(5946761378348435037)
XLA Ops:
  0.0 50.8 %fisher.1 = (bf16[8,4,2,2,2,96,256]{6,5,4,3,2,1,0:T(8,128)(2,1)S(1)}, bf16[8,768,256]{2,1,0:T(8,128)(2,1)S(1)}, f32[768,1536]{1,0:T(8,128)S(1)}) custom-call(bf16[256,96]{1,0:T(8,128)(2,1)} %bitcast.7, s32[1,96]{1,0:T(1,128)} %bitcast.8, f32[8]{0:T(128)} %scale_in.1, f32[2,2]{1,0:T(2,128)} %coupling_in.1, f32[3,4]{1,0:T(4,128)} %second_in.1, ...), custom_call_target="tpu_custom_call" | custom-call | flops 4831838208 | bytes 10000000 | tf_op jit(solution)/shard_map/fisher/pallas_call | solution.py:473
  50.9 6.3 %finish.1 = f32[768,3072]{1,0:T(8,128)} custom-call(bf16[8,4,2,2,2,96,256]{6,5,4,3,2,1,0:T(8,128)(2,1)S(1)} %get-tuple-element.8.panels, bf16[8,768,256]{2,1,0:T(8,128)(2,1)S(1)} %get-tuple-element.9.weights, f32[768,1536]{1,0:T(8,128)S(1)} %get-tuple-element.10.head), custom_call_target="tpu_custom_call" | custom-call | flops 4831838208 | bytes 10000000 | tf_op jit(solution)/shard_map/finish/pallas_call | solution.py:524

commit v3 on v2

--- a/solution.py
+++ b/solution.py
@@ -17,10 +17,10 @@
 GROUPS = ((0, 1), (1, 2), (3, 2), (5, 2), (7, 1))
 GROUP_OF = (0, 1, 1, 2, 2, 3, 3, 4)
 WIDE = 512
-PART = {"A": (0, 32), "B": (32, 32), "C": (64, 32), "BC": (32, 64)}
-
-
-HEAD = 1536
+PART = {"A": (0, 32),  "B": (32, 32), "C": (64, 32), "BC": (32, 64)}
+
+
+HEAD = 2048
 
 
 def events():
@@ -34,7 +34,7 @@
     for g in range(5):
         out += [f"by{g}", f"cx{g}", f"bf{g}", f"cf{g}"]
         out += [f"{n}{g}{w}" for n in ("bx", "cy") for w in "+-"]
-        out += [f"core{p}{g}" for p in "ABC"]
+        out += [f"core{p}{g}" for p in "ANF"]
     return {n: i for i, n in enumerate(out)}
 
 
@@ -53,8 +53,8 @@
     return out
 
 
-def product(weights, panels, i):
-    lhs = jnp.concatenate([weights[t] for t in range(8)], axis=1)
+def product(weights, panels, i, row=0, height=8 * OWN):
+    lhs = jnp.concatenate([weights[t, row : row + height] for t in range(8)], axis=1)
     blocks = []
     for slot, (inner, size) in slots(i).items():
         block = [panels[slot, t // 2, t % 2].reshape(4 * OWN, ROWS) for t in range(8)]
@@ -67,27 +67,32 @@
 def finish(panels, weights, head, out_ref, tail, sems):
     z = lax.div(lax.axis_index("nuis"), 4)
     copies = []
-
-    def write(i, source, first):
+    half = 4 * OWN
+
+    def write(i, source, first, row=0, height=8 * OWN):
         at = first
         for slot, (inner, size) in slots(i).items():
             column = lax.rem(z + (DISTANCE[slot] + 8), 8) * 384 + inner
             copy = pltpu.make_async_copy(
-                source.at[:, pl.ds(at, size)],
-                out_ref.at[:, pl.ds(pl.multiple_of(column, 128), size)],
+                source.at[pl.ds(row, height), pl.ds(at, size)],
+                out_ref.at[pl.ds(row, height), pl.ds(pl.multiple_of(column, 128), size)],
                 sems.at[len(copies)],
             )
             copy.start()
             copies.append(copy)
             at += size
 
-    for i in range(6):
-        if i < HEAD // WIDE:
-            write(i, head, i * WIDE)
-        else:
-            tail[:, i * WIDE - HEAD : (i + 1) * WIDE - HEAD] = product(weights, panels, i)
-            write(i, tail, i * WIDE - HEAD)
-    for copy in copies:
+    for i in range(HEAD // WIDE):
+        write(i, head, i * WIDE)
+    waited = 0
+    for i in range(HEAD // WIDE, 6):
+        first = i * WIDE - HEAD
+        for row in (0, half):
+            tail[row : row + half, first : first + WIDE] = product(weights, panels, i, row, half)
+            write(i, tail, first, row, half)
+            copies[waited].wait()
+            waited += 1
+    for copy in copies[waited:]:
         copy.wait()
 
 
@@ -156,7 +161,7 @@
         copy.start()
 
     partners = [dict(dx=dx, dy=dy) for dx in range(4) for dy in range(4) if dx or dy]
-    partners += [dict(dz=1), dict(dz=-1), dict(dc=1)]
+    partners += [dict(dz=dz) for dz in range(1, 8)] + [dict(dc=1)]
     barrier = pltpu.get_barrier_semaphore()
     for p in partners:
         pl.semaphore_signal(barrier, inc=1, device_id=device(**p), device_id_type=MESH)
@@ -233,6 +238,10 @@
                 empty(semaphore, rows(480))
             elif e[:2] in ("by", "cx"):
                 empty(semaphore, rows(96 * GROUPS[int(e[2])][1]))
+            elif e.startswith("coreN"):
+                empty(semaphore, rows(768, GROUPS[int(e[5])][1]))
+            elif e.startswith("coreF"):
+                empty(semaphore, rows(256 * GROUPS[int(e[5])][1]))
             elif e[:2] in ("bf", "cf"):
                 empty(semaphore, rows(128 * GROUPS[int(e[2])][1]))
             else:
@@ -241,6 +250,16 @@
     nb, pb = lax.rem(b + 1, 8), lax.rem(b + 7, 8)
     send("halo+", "halo+", deriv_ref.at[pl.ds(CELLS, CELLS)], halo.at[0], (nb, n))
     send("halo-", "halo-", deriv_ref.at[pl.ds(0, CELLS)], halo.at[1], (pb, n))
+    for o in range(1, 8):
+        peer = lax.rem(b + o, 8)
+        send(
+            "exp",
+            "exp",
+            exp_ref.at[pl.ds(pl.multiple_of(peer * 8, 8), 8)],
+            expected.at[b],
+            (peer, n),
+        )
+    expected[b] = exp_ref[pl.ds(pl.multiple_of(b * 8, 8), 8), :]
     first = deriv_ref[pl.ds(0, CELLS), :].astype(jnp.float32)
     second = deriv_ref[pl.ds(CELLS, CELLS), :].astype(jnp.float32)
     low0 = jnp.where(b == 0, 0.0, coupling_ref[0, 0])
@@ -263,35 +282,19 @@
         )
         panels[0, x, yh, yl, c, :, a * CELLS : (a + 1) * CELLS] = panel.T.astype(jnp.bfloat16)
 
-    def send_expected():
-        for o in range(1, 8):
-            peer = lax.rem(b + o, 8)
-            send(
-                "exp",
-                "exp",
-                exp_ref.at[pl.ds(pl.multiple_of(peer * 8, 8), 8)],
-                expected.at[b],
-                (peer, n),
-            )
-        expected[b] = exp_ref[pl.ds(pl.multiple_of(b * 8, 8), 8), :]
-
     def own(slots, part, *place):
         lo, size = PART[part]
         return panels.at[(slots, *place, pl.ds(lo, size))]
 
-    def z_step(s):
+    def along_z(s):
         for w, sign in (("+", 1), ("-", -1)):
-            if s > 1:
-                need(f"z{s - 1}{w}")
             part = "BC" if s < 4 else ("B" if sign == 1 else "C")
-            src = SLOT[-sign * (s - 1)]
-            dst = SLOT[-sign * s]
             send(
                 f"z{s}{w}",
                 "z",
-                own(src, part, x, yh, yl, c),
-                own(dst, part, x, yh, yl, c),
-                device(dz=sign),
+                own(0, part, x, yh, yl, c),
+                own(SLOT[-sign * s], part, x, yh, yl, c),
+                device(dz=sign * s),
             )
 
     def group(g):
@@ -360,13 +363,22 @@
         else:
             need(*[e for e in EVENTS if e.startswith(f"az{g}")])
 
-    def share_bc(g):
+    def share_near(g):
+        for d in (0, 1, 3):
+            line = own(group(g), "B", lax.rem(x + d, 4), slice(None), slice(None), c)
+            send(f"coreN{g}", f"core{g}", line, line, device(dc=1))
+            oy = lax.rem(y + d, 4)
+            line = own(group(g), "C", slice(None), lax.div(oy, 2), lax.rem(oy, 2), c)
+            send(f"coreN{g}", f"core{g}", line, line, device(dc=1))
+
+    def share_far(g):
         need(f"bf{g}")
-        block = own(group(g), "B", slice(None), slice(None), slice(None), c)
-        send(f"coreB{g}", f"core{g}", block, block, device(dc=1))
+        line = own(group(g), "B", lax.rem(x + 2, 4), slice(None), slice(None), c)
+        send(f"coreF{g}", f"core{g}", line, line, device(dc=1))
         need(f"cf{g}")
-        block = own(group(g), "C", slice(None), slice(None), slice(None), c)
-        send(f"coreC{g}", f"core{g}", block, block, device(dc=1))
+        oy = lax.rem(y + 2, 4)
+        line = own(group(g), "C", slice(None), lax.div(oy, 2), lax.rem(oy, 2), c)
+        send(f"coreF{g}", f"core{g}", line, line, device(dc=1))
 
     def share_a(g):
         own_a(g)
@@ -389,54 +401,59 @@
 
     def multiply(i):
         for slot in slots(i):
-            need(*[f"core{p}{GROUP_OF[slot]}" for p in "ABC"])
+            need(*[f"core{p}{GROUP_OF[slot]}" for p in "ANF"])
         out_ref[:, i * WIDE : (i + 1) * WIDE] = product(weights, panels, i)
 
-    z_step(1)
+    along_z(1)
     first_axis(0)
     plane_a()
-    z_step(2)
+    along_z(2)
+    along_z(3)
+    along_z(4)
     first_axis(1)
     second_axis(0)
-    z_step(3)
+    first_axis(2)
+    first_axis(3)
     ring_a(1, 0)
-    first_axis(2)
     ring_a(1, 1)
+    first_axis(4)
     second_axis(1)
     far(0)
-    send_expected()
-    z_step(4)
-    first_axis(3)
+    share_near(0)
     share_a(0)
     second_axis(2)
+    ring_a(2, 0)
+    ring_a(2, 1)
     far(1)
-    ring_a(2, 0)
-    first_axis(4)
     second_axis(3)
-    share_bc(0)
-    ring_a(2, 1)
+    share_near(1)
+    share_far(0)
+    share_a(1)
     weigh()
-    share_a(1)
+    ring_a(3, 0)
     far(2)
     second_axis(4)
-    ring_a(3, 0)
-    share_bc(1)
+    share_near(2)
+    share_far(1)
     ring_a(3, 1)
     far(3)
+    ring_a(4, 0)
+    share_near(3)
+    share_a(2)
     multiply(0)
-    share_a(2)
-    ring_a(4, 0)
-    share_bc(2)
+    share_far(2)
     far(4)
+    ring_a(4, 1)
+    share_near(4)
+    share_a(3)
     multiply(1)
-    ring_a(4, 1)
-    share_a(3)
-    share_bc(3)
+    share_far(3)
     multiply(2)
-    share_bc(4)
+    share_far(4)
     share_a(4)
+    multiply(3)
     for g in range(5):
-        need(*[f"core{p}{g}" for p in "ABC"])
+        need(*[f"core{p}{g}" for p in "ANF"])
     for d in DEPARTURES:
         semaphore = send_sem.at[DEPARTURES[d]]
         if d == "exp":
@@ -528,7 +545,7 @@
         out_specs=hbm,
         scratch_shapes=[
             pltpu.VMEM((8 * OWN, 3072 - HEAD), jnp.float32),
-            pltpu.SemaphoreType.DMA((16,)),
+            pltpu.SemaphoreType.DMA((24,)),
         ],
         compiler_params=pltpu.CompilerParams(vmem_limit_bytes=16 * 1024 * 1024),
         cost_estimate=pl.CostEstimate(

time: 57.3 us -> 53.7 us (0.937)
  Pallas kernels: 57.2 us -> 53.6 us
    pallas_call x1, Pallas kernels: 50.8 us -> 48.5 us  [local(): pl.pallas_call(kernel, out_shape=[pltpu.VMEM((8, 4, 2, 2, 2, OWN, ROWS),...]
    pallas_call x1, Pallas kernels: 6.34 us -> 5.16 us  [local(): pl.pallas_call(finish, out_shape=jax.ShapeDtypeStruct((8 * OWN, 3072), jn...]
where the time goes in v3:
time: 53.7 us; the launch traced here: 53.6 us
  Pallas kernels  53.6 us (100%)
    pallas_call x1, Pallas kernels, local(): pl.pallas_call(kernel, out_shape=[pltpu.VMEM((8, 4, 2, 2, 2, OWN, ROWS),...  48.5 us
    pallas_call x1, Pallas kernels, local(): pl.pallas_call(finish, out_shape=jax.ShapeDtypeStruct((8 * OWN, 3072), jn...  5.16 us

profile of v3, /device:TPU:1, one launch (start us, length us, event | category | flops | bytes accessed | tf_op | source)
XLA Modules:
  0.0 53.6 jit_solution(148138809632431013)
XLA Ops:
  0.0 48.5 %fisher.1 = (bf16[8,4,2,2,2,96,256]{6,5,4,3,2,1,0:T(8,128)(2,1)S(1)}, bf16[8,768,256]{2,1,0:T(8,128)(2,1)S(1)}, f32[768,2048]{1,0:T(8,128)S(1)}) custom-call(bf16[256,96]{1,0:T(8,128)(2,1)} %bitcast.7, s32[1,96]{1,0:T(1,128)} %bitcast.8, f32[8]{0:T(128)} %scale_in.1, f32[2,2]{1,0:T(2,128)} %coupling_in.1, f32[3,4]{1,0:T(4,128)} %second_in.1, ...), custom_call_target="tpu_custom_call" | custom-call | flops 6442450944 | bytes 10000000 | tf_op jit(solution)/shard_map/fisher/pallas_call | solution.py:490
  48.5 5.2 %finish.1 = f32[768,3072]{1,0:T(8,128)} custom-call(bf16[8,4,2,2,2,96,256]{6,5,4,3,2,1,0:T(8,128)(2,1)S(1)} %get-tuple-element.8.panels, bf16[8,768,256]{2,1,0:T(8,128)(2,1)S(1)} %get-tuple-element.9.weights, f32[768,2048]{1,0:T(8,128)S(1)} %get-tuple-element.10.head), custom_call_target="tpu_custom_call" | custom-call | flops 3221225472 | bytes 10000000 | tf_op jit(solution)/shard_map/finish/pallas_call | solution.py:541

commit v4 on v3

--- a/solution.py
+++ b/solution.py
@@ -17,31 +17,38 @@
 GROUPS = ((0, 1), (1, 2), (3, 2), (5, 2), (7, 1))
 GROUP_OF = (0, 1, 1, 2, 2, 3, 3, 4)
 WIDE = 512
-PART = {"A": (0, 32),  "B": (32, 32), "C": (64, 32), "BC": (32, 64)}
+PART = {"A": (0, 32),  "B": (32, 32), "C": (64, 32), "B0": (32, 16), "B1": (48, 16), "C0": (64, 16), "C1": (80, 16), "BC": (32, 64)}
 
 
 HEAD = 2048
 
 
+def ring_signs(s, h):
+    return (1, -1) if s < 4 else ((1,), (-1,))[h]
+
+
 def events():
-    out = ["halo+", "halo-", "exp", "ap"]
-    out += [f"z{s}{w}" for s in range(1, 5) for w in "+-"]
+    out = {"halo+": 0, "halo-": 0, "exp": 0, "ap": 480}
     for s in range(1, 5):
-        for w in "+-":
-            for h in range(2):
-                if s < 4 or h == (0 if w == "+" else 1):
-                    out.append(f"az{s}{w}{h}")
-    for g in range(5):
-        out += [f"by{g}", f"cx{g}", f"bf{g}", f"cf{g}"]
-        out += [f"{n}{g}{w}" for n in ("bx", "cy") for w in "+-"]
-        out += [f"core{p}{g}" for p in "ANF"]
-    return {n: i for i, n in enumerate(out)}
-
-
-EVENTS = events()
-DEPARTURES = ["halo+", "halo-", "exp", "ap", "z", "az"]
-DEPARTURES += [f"{n}{g}" for n in ("link", "core") for g in range(5)]
-DEPARTURES = {n: i for i, n in enumerate(DEPARTURES)}
+        out[f"z{s}"] = 128 if s < 4 else 64
+        for h in range(2):
+            for sign in ring_signs(s, h):
+                out[f"az{s}{h}{sign}"] = 256
+    for g, (_, n) in enumerate(GROUPS):
+        if g in RELAYED:
+            out[f"near{g}"], out[f"relay{g}"] = 128 * n, 64 * n
+        else:
+            out[f"first{g}"] = 192 * n
+        for sign in (1, -1):
+            out[f"bx{g}{sign}"] = out[f"cy{g}{sign}"] = 128 * n
+        out[f"far{g}"], out[f"core{g}"] = 256 * n, 1536 * n
+    return out
+
+
+RELAYED = (3, 4)
+COUNTS = events()
+EVENTS = {n: i for i, n in enumerate(COUNTS)}
+DEPARTURES = {n: i for i, n in enumerate(("halo+", "halo-", "exp", "ap", "z", "az", "link", "core"))}
 
 
 def slots(i):
@@ -66,34 +73,36 @@
 
 def finish(panels, weights, head, out_ref, tail, sems):
     z = lax.div(lax.axis_index("nuis"), 4)
-    copies = []
     half = 4 * OWN
 
-    def write(i, source, first, row=0, height=8 * OWN):
+    def write(i, source, first, semaphore, row=0, height=8 * OWN):
         at = first
         for slot, (inner, size) in slots(i).items():
             column = lax.rem(z + (DISTANCE[slot] + 8), 8) * 384 + inner
-            copy = pltpu.make_async_copy(
+            pltpu.make_async_copy(
                 source.at[pl.ds(row, height), pl.ds(at, size)],
                 out_ref.at[pl.ds(row, height), pl.ds(pl.multiple_of(column, 128), size)],
-                sems.at[len(copies)],
-            )
-            copy.start()
-            copies.append(copy)
+                semaphore,
+            ).start()
             at += size
 
-    for i in range(HEAD // WIDE):
-        write(i, head, i * WIDE)
-    waited = 0
-    for i in range(HEAD // WIDE, 6):
+    def written(semaphore, height=8 * OWN):
+        block = head.at[pl.ds(0, height), pl.ds(0, WIDE)]
+        pltpu.make_async_copy(block, block, semaphore).wait()
+
+    early = HEAD // WIDE
+    for i in range(early):
+        write(i, head, i * WIDE, sems.at[i])
+    step = 0
+    for i in range(early, 6):
         first = i * WIDE - HEAD
         for row in (0, half):
             tail[row : row + half, first : first + WIDE] = product(weights, panels, i, row, half)
-            write(i, tail, first, row, half)
-            copies[waited].wait()
-            waited += 1
-    for copy in copies[waited:]:
-        copy.wait()
+            write(i, tail, first, sems.at[early + step], row, half)
+            written(sems.at[step])
+            step += 1
+    for i in range(step):
+        written(sems.at[early + i], half)
 
 
 def kernel(
@@ -207,8 +216,11 @@
     departed = {}
     arrived = set()
 
-    def rows(count, wide=1):
-        return weights.at[pl.ds(0, wide), pl.ds(0, count)]
+    def rows(count):
+        wide = 1
+        while count // wide > 8 * OWN:
+            wide *= 2
+        return weights.at[pl.ds(0, wide), pl.ds(0, count // wide)]
 
     def send(event, departure, src, dst, target):
         copy = pltpu.make_async_remote_copy(
@@ -234,16 +246,8 @@
             semaphore = recv_sem.at[EVENTS[e]]
             if e == "exp":
                 empty(semaphore, expected.at[pl.ds(0, 7)])
-            elif e == "ap":
-                empty(semaphore, rows(480))
-            elif e[:2] in ("by", "cx"):
-                empty(semaphore, rows(96 * GROUPS[int(e[2])][1]))
-            elif e.startswith("coreN"):
-                empty(semaphore, rows(768, GROUPS[int(e[5])][1]))
-            elif e.startswith("coreF"):
-                empty(semaphore, rows(256 * GROUPS[int(e[5])][1]))
-            elif e[:2] in ("bf", "cf"):
-                empty(semaphore, rows(128 * GROUPS[int(e[2])][1]))
+            elif COUNTS[e]:
+                empty(semaphore, rows(COUNTS[e]))
             else:
                 started[e].wait_recv()
 
@@ -290,7 +294,7 @@
         for w, sign in (("+", 1), ("-", -1)):
             part = "BC" if s < 4 else ("B" if sign == 1 else "C")
             send(
-                f"z{s}{w}",
+                f"z{s}",
                 "z",
                 own(0, part, x, yh, yl, c),
                 own(SLOT[-sign * s], part, x, yh, yl, c),
@@ -300,38 +304,45 @@
     def group(g):
         return pl.ds(*GROUPS[g])
 
-    def group_here(g):
-        if 1 <= g:
-            need(f"z{g}+", f"z{g}-")
-
     def first_axis(g):
-        group_here(g)
+        if g:
+            need(f"z{g}")
         mine_b = own(group(g), "B", x, yh, yl, c)
         mine_c = own(group(g), "C", x, yh, yl, c)
-        for d in (1, 3, 2):
-            send(f"by{g}", f"link{g}", mine_b, mine_b, device(dy=d))
-            send(f"cx{g}", f"link{g}", mine_c, mine_c, device(dx=d))
+        event = f"near{g}" if g in RELAYED else f"first{g}"
+        for d in (1, 3) if g in RELAYED else (1, 3, 2):
+            send(event, "link", mine_b, mine_b, device(dy=d))
+            send(event, "link", mine_c, mine_c, device(dx=d))
+
+    def relay(g):
+        need(f"near{g}")
+        for half, sign in (("0", 1), ("1", -1)):
+            oy = lax.rem(y + (4 - sign), 4)
+            piece = own(group(g), "B" + half, x, lax.div(oy, 2), lax.rem(oy, 2), c)
+            send(f"relay{g}", "link", piece, piece, device(dy=sign))
+            piece = own(group(g), "C" + half, lax.rem(x + (4 - sign), 4), yh, yl, c)
+            send(f"relay{g}", "link", piece, piece, device(dx=sign))
 
     def second_axis(g):
-        need(f"by{g}")
-        line = own(group(g), "B", x, slice(None), slice(None), c)
-        for w, sign in (("+", 1), ("-", -1)):
-            send(f"bx{g}{w}", f"link{g}", line, line, device(dx=sign))
-        need(f"cx{g}")
-        line = own(group(g), "C", slice(None), yh, yl, c)
-        for w, sign in (("+", 1), ("-", -1)):
-            send(f"cy{g}{w}", f"link{g}", line, line, device(dy=sign))
+        if g in RELAYED:
+            need(f"near{g}", f"relay{g}")
+        else:
+            need(f"first{g}")
+        row = own(group(g), "B", x, slice(None), slice(None), c)
+        column = own(group(g), "C", slice(None), yh, yl, c)
+        for sign in (1, -1):
+            send(f"bx{g}{sign}", "link", row, row, device(dx=sign))
+            send(f"cy{g}{sign}", "link", column, column, device(dy=sign))
 
     def far(g):
-        for w, sign in (("+", 1), ("-", -1)):
-            need(f"bx{g}{w}")
-            line = own(group(g), "B", lax.rem(x + (4 - sign), 4), 0 if sign == 1 else 1, slice(None), c)
-            send(f"bf{g}", f"link{g}", line, line, device(dx=sign))
-        for w, sign in (("+", 1), ("-", -1)):
-            need(f"cy{g}{w}")
+        for i, sign in enumerate((1, -1)):
+            need(f"bx{g}{sign}")
+            line = own(group(g), "B", lax.rem(x + (4 - sign), 4), i, slice(None), c)
+            send(f"far{g}", "link", line, line, device(dx=sign))
+            need(f"cy{g}{sign}")
             oy = lax.rem(y + (4 - sign), 4)
-            line = own(group(g), "C", pl.ds(0 if sign == 1 else 2, 2), lax.div(oy, 2), lax.rem(oy, 2), c)
-            send(f"cf{g}", f"link{g}", line, line, device(dy=sign))
+            line = own(group(g), "C", pl.ds(2 * i, 2), lax.div(oy, 2), lax.rem(oy, 2), c)
+            send(f"far{g}", "link", line, line, device(dy=sign))
 
     def plane_a():
         mine = own(0, "A", x, yh, yl, c)
@@ -341,16 +352,11 @@
                     send("ap", "ap", mine, mine, device(dx=dx, dy=dy))
 
     def ring_a(s, h):
-        for w, sign in (("+", 1), ("-", -1)):
-            if f"az{s}{w}{h}" not in EVENTS:
-                continue
-            if s > 1:
-                need(f"az{s - 1}{w}{h}")
-            else:
-                need("ap")
-            place = (pl.ds(2 * h, 2), slice(None), slice(None), c)
+        place = (pl.ds(2 * h, 2), slice(None), slice(None), c)
+        for sign in ring_signs(s, h):
+            need("ap" if s == 1 else f"az{s - 1}{h}{sign}")
             send(
-                f"az{s}{w}{h}",
+                f"az{s}{h}{sign}",
                 "az",
                 own(SLOT[-sign * (s - 1)], "A", *place),
                 own(SLOT[-sign * s], "A", *place),
@@ -361,29 +367,28 @@
         if g == 0:
             need("ap")
         else:
-            need(*[e for e in EVENTS if e.startswith(f"az{g}")])
+            need(*[f"az{g}{h}{sign}" for h in range(2) for sign in ring_signs(g, h)])
 
     def share_near(g):
         for d in (0, 1, 3):
             line = own(group(g), "B", lax.rem(x + d, 4), slice(None), slice(None), c)
-            send(f"coreN{g}", f"core{g}", line, line, device(dc=1))
+            send(f"core{g}", "core", line, line, device(dc=1))
             oy = lax.rem(y + d, 4)
             line = own(group(g), "C", slice(None), lax.div(oy, 2), lax.rem(oy, 2), c)
-            send(f"coreN{g}", f"core{g}", line, line, device(dc=1))
+            send(f"core{g}", "core", line, line, device(dc=1))
 
     def share_far(g):
-        need(f"bf{g}")
+        need(f"far{g}")
         line = own(group(g), "B", lax.rem(x + 2, 4), slice(None), slice(None), c)
-        send(f"coreF{g}", f"core{g}", line, line, device(dc=1))
-        need(f"cf{g}")
+        send(f"core{g}", "core", line, line, device(dc=1))
         oy = lax.rem(y + 2, 4)
         line = own(group(g), "C", slice(None), lax.div(oy, 2), lax.rem(oy, 2), c)
-        send(f"coreF{g}", f"core{g}", line, line, device(dc=1))
+        send(f"core{g}", "core", line, line, device(dc=1))
 
     def share_a(g):
         own_a(g)
         block = own(group(g), "A", slice(None), slice(None), slice(None), c)
-        send(f"coreA{g}", f"core{g}", block, block, device(dc=1))
+        send(f"core{g}", "core", block, block, device(dc=1))
 
     def weigh():
         need("exp")
@@ -401,7 +406,7 @@
 
     def multiply(i):
         for slot in slots(i):
-            need(*[f"core{p}{GROUP_OF[slot]}" for p in "ANF"])
+            need(f"core{GROUP_OF[slot]}")
         out_ref[:, i * WIDE : (i + 1) * WIDE] = product(weights, panels, i)
 
     along_z(1)
@@ -421,7 +426,9 @@
     far(0)
     share_near(0)
     share_a(0)
+    relay(3)
     second_axis(2)
+    relay(4)
     ring_a(2, 0)
     ring_a(2, 1)
     far(1)
@@ -453,9 +460,9 @@
     share_a(4)
     multiply(3)
     for g in range(5):
-        need(*[f"core{p}{g}" for p in "ANF"])
-    for d in DEPARTURES:
-        semaphore = send_sem.at[DEPARTURES[d]]
+        need(f"core{g}")
+    for d, i in DEPARTURES.items():
+        semaphore = send_sem.at[i]
         if d == "exp":
             empty(semaphore, expected.at[pl.ds(0, 7)])
         elif d == "ap":
@@ -463,11 +470,11 @@
         elif d == "z":
             empty(semaphore, rows(448))
         elif d == "az":
-            empty(semaphore, rows(512, 7))
-        elif d.startswith("link"):
-            empty(semaphore, rows(480, 2 * GROUPS[int(d[4])][1]))
-        elif d.startswith("core"):
-            empty(semaphore, panels.at[group(int(d[4])), :, :, :, 0])
+            empty(semaphore, rows(3584))
+        elif d == "link":
+            empty(semaphore, panels.at[pl.ds(0, 5), :, :, :, 0])
+        elif d == "core":
+            empty(semaphore, panels.at[pl.ds(0, 4)])
         else:
             departed[d].wait_send()
 
@@ -545,7 +552,7 @@
         out_specs=hbm,
         scratch_shapes=[
             pltpu.VMEM((8 * OWN, 3072 - HEAD), jnp.float32),
-            pltpu.SemaphoreType.DMA((24,)),
+            pltpu.SemaphoreType.DMA((8,)),
         ],
         compiler_params=pltpu.CompilerParams(vmem_limit_bytes=16 * 1024 * 1024),
         cost_estimate=pl.CostEstimate(

time: 53.7 us -> 53.7 us (level)
  no operation moved by 1% of the time
where the time goes in v4:
time: 53.7 us; the launch traced here: 53.6 us
  Pallas kernels  53.6 us (100%)
    pallas_call x1, Pallas kernels, local(): pl.pallas_call(kernel, out_shape=[pltpu.VMEM((8, 4, 2, 2, 2, OWN, ROWS),...  48.5 us
    pallas_call x1, Pallas kernels, local(): pl.pallas_call(finish, out_shape=jax.ShapeDtypeStruct((8 * OWN, 3072), jn...  5.14 us

profile of v4, /device:TPU:1, one launch (start us, length us, event | category | flops | bytes accessed | tf_op | source)
XLA Modules:
  0.0 53.6 jit_solution(14933401001363140355)
XLA Ops:
  0.0 48.5 %fisher.1 = (bf16[8,4,2,2,2,96,256]{6,5,4,3,2,1,0:T(8,128)(2,1)S(1)}, bf16[8,768,256]{2,1,0:T(8,128)(2,1)S(1)}, f32[768,2048]{1,0:T(8,128)S(1)}) custom-call(bf16[256,96]{1,0:T(8,128)(2,1)} %bitcast.7, s32[1,96]{1,0:T(1,128)} %bitcast.8, f32[8]{0:T(128)} %scale_in.1, f32[2,2]{1,0:T(2,128)} %coupling_in.1, f32[3,4]{1,0:T(4,128)} %second_in.1, ...), custom_call_target="tpu_custom_call" | custom-call | flops 6442450944 | bytes 10000000 | tf_op jit(solution)/shard_map/fisher/pallas_call | solution.py:497
  48.5 5.1 %finish.1 = f32[768,3072]{1,0:T(8,128)} custom-call(bf16[8,4,2,2,2,96,256]{6,5,4,3,2,1,0:T(8,128)(2,1)S(1)} %get-tuple-element.8.panels, bf16[8,768,256]{2,1,0:T(8,128)(2,1)S(1)} %get-tuple-element.9.weights, f32[768,2048]{1,0:T(8,128)S(1)} %get-tuple-element.10.head), custom_call_target="tpu_custom_call" | custom-call | flops 3221225472 | bytes 10000000 | tf_op jit(solution)/shard_map/finish/pallas_call | solution.py:548

commit v5 on v4

--- a/solution.py
+++ b/solution.py
@@ -175,8 +175,64 @@
     for p in partners:
         pl.semaphore_signal(barrier, inc=1, device_id=device(**p), device_id_type=MESH)
 
-    for copy in inputs[:6]:
+    inputs[8].wait()
+    pl.semaphore_wait(barrier, len(partners))
+
+    started = {}
+    departed = {}
+    arrived = set()
+
+    def rows(count):
+        wide = 1
+        while count // wide > 8 * OWN:
+            wide *= 2
+        return weights.at[pl.ds(0, wide), pl.ds(0, count // wide)]
+
+    def send(event, departure, src, dst, target):
+        copy = pltpu.make_async_remote_copy(
+            src_ref=src,
+            dst_ref=dst,
+            send_sem=send_sem.at[DEPARTURES[departure]],
+            recv_sem=recv_sem.at[EVENTS[event]],
+            device_id=target,
+            device_id_type=MESH,
+        )
+        copy.start()
+        started[event] = copy
+        departed[departure] = copy
+
+    def empty(semaphore, like):
+        pltpu.make_async_copy(like, like, semaphore).wait()
+
+    def need(*events):
+        for e in events:
+            if e in arrived:
+                continue
+            arrived.add(e)
+            semaphore = recv_sem.at[EVENTS[e]]
+            if e == "exp":
+                empty(semaphore, expected.at[pl.ds(0, 7)])
+            elif COUNTS[e]:
+                empty(semaphore, rows(COUNTS[e]))
+            else:
+                started[e].wait_recv()
+
+    nb, pb = lax.rem(b + 1, 8), lax.rem(b + 7, 8)
+    send("halo+", "halo+", deriv_ref.at[pl.ds(CELLS, CELLS)], halo.at[0], (nb, n))
+    send("halo-", "halo-", deriv_ref.at[pl.ds(0, CELLS)], halo.at[1], (pb, n))
+    for copy in inputs[:8]:
         copy.wait()
+    exp_ref[...] = exp_cols[...].T
+    for o in range(1, 8):
+        peer = lax.rem(b + o, 8)
+        send(
+            "exp",
+            "exp",
+            exp_ref.at[pl.ds(pl.multiple_of(peer * 8, 8), 8)],
+            expected.at[b],
+            (peer, n),
+        )
+    expected[b] = exp_ref[pl.ds(pl.multiple_of(b * 8, 8), 8), :]
     row = lax.broadcasted_iota(jnp.int32, (CELLS, CELLS), 0)
     col = lax.broadcasted_iota(jnp.int32, (CELLS, CELLS), 1)
     zero = jnp.zeros((CELLS, CELLS), jnp.float32)
@@ -207,63 +263,6 @@
     for g in range(8):
         gain = jnp.where(ids == g, scale_ref[g], gain)
     gain_ref[...] = gain
-    for copy in inputs[6:]:
-        copy.wait()
-    exp_ref[...] = exp_cols[...].T
-    pl.semaphore_wait(barrier, len(partners))
-
-    started = {}
-    departed = {}
-    arrived = set()
-
-    def rows(count):
-        wide = 1
-        while count // wide > 8 * OWN:
-            wide *= 2
-        return weights.at[pl.ds(0, wide), pl.ds(0, count // wide)]
-
-    def send(event, departure, src, dst, target):
-        copy = pltpu.make_async_remote_copy(
-            src_ref=src,
-            dst_ref=dst,
-            send_sem=send_sem.at[DEPARTURES[departure]],
-            recv_sem=recv_sem.at[EVENTS[event]],
-            device_id=target,
-            device_id_type=MESH,
-        )
-        copy.start()
-        started[event] = copy
-        departed[departure] = copy
-
-    def empty(semaphore, like):
-        pltpu.make_async_copy(like, like, semaphore).wait()
-
-    def need(*events):
-        for e in events:
-            if e in arrived:
-                continue
-            arrived.add(e)
-            semaphore = recv_sem.at[EVENTS[e]]
-            if e == "exp":
-                empty(semaphore, expected.at[pl.ds(0, 7)])
-            elif COUNTS[e]:
-                empty(semaphore, rows(COUNTS[e]))
-            else:
-                started[e].wait_recv()
-
-    nb, pb = lax.rem(b + 1, 8), lax.rem(b + 7, 8)
-    send("halo+", "halo+", deriv_ref.at[pl.ds(CELLS, CELLS)], halo.at[0], (nb, n))
-    send("halo-", "halo-", deriv_ref.at[pl.ds(0, CELLS)], halo.at[1], (pb, n))
-    for o in range(1, 8):
-        peer = lax.rem(b + o, 8)
-        send(
-            "exp",
-            "exp",
-            exp_ref.at[pl.ds(pl.multiple_of(peer * 8, 8), 8)],
-            expected.at[b],
-            (peer, n),
-        )
-    expected[b] = exp_ref[pl.ds(pl.multiple_of(b * 8, 8), 8), :]
     first = deriv_ref[pl.ds(0, CELLS), :].astype(jnp.float32)
     second = deriv_ref[pl.ds(CELLS, CELLS), :].astype(jnp.float32)
     low0 = jnp.where(b == 0, 0.0, coupling_ref[0, 0])

time: 53.7 us -> 53.7 us (level)
  no operation moved by 1% of the time
where the time goes in v5:
time: 53.7 us; the launch traced here: 53.6 us
  Pallas kernels  53.6 us (100%)
    pallas_call x1, Pallas kernels, local(): pl.pallas_call(kernel, out_shape=[pltpu.VMEM((8, 4, 2, 2, 2, OWN, ROWS),...  48.5 us
    pallas_call x1, Pallas kernels, local(): pl.pallas_call(finish, out_shape=jax.ShapeDtypeStruct((8 * OWN, 3072), jn...  5.13 us

profile of v5, /device:TPU:1, one launch (start us, length us, event | category | flops | bytes accessed | tf_op | source)
XLA Modules:
  0.0 53.6 jit_solution(1958024521098749283)
XLA Ops:
  0.0 48.5 %fisher.1 = (bf16[8,4,2,2,2,96,256]{6,5,4,3,2,1,0:T(8,128)(2,1)S(1)}, bf16[8,768,256]{2,1,0:T(8,128)(2,1)S(1)}, f32[768,2048]{1,0:T(8,128)S(1)}) custom-call(bf16[256,96]{1,0:T(8,128)(2,1)} %bitcast.7, s32[1,96]{1,0:T(1,128)} %bitcast.8, f32[8]{0:T(128)} %scale_in.1, f32[2,2]{1,0:T(2,128)} %coupling_in.1, f32[3,4]{1,0:T(4,128)} %second_in.1, ...), custom_call_target="tpu_custom_call" | custom-call | flops 6442450944 | bytes 10000000 | tf_op jit(solution)/shard_map/fisher/pallas_call | solution.py:496
  48.5 5.1 %finish.1 = f32[768,3072]{1,0:T(8,128)} custom-call(bf16[8,4,2,2,2,96,256]{6,5,4,3,2,1,0:T(8,128)(2,1)S(1)} %get-tuple-element.8.panels, bf16[8,768,256]{2,1,0:T(8,128)(2,1)S(1)} %get-tuple-element.9.weights, f32[768,2048]{1,0:T(8,128)S(1)} %get-tuple-element.10.head), custom_call_target="tpu_custom_call" | custom-call | flops 3221225472 | bytes 10000000 | tf_op jit(solution)/shard_map/finish/pallas_call | solution.py:547
